TPU v7x, 32 devices: a whole 2x2x4 slice. The times are simulated.
32 devices in a mesh: pp: 2 (over x), cp: 4 (over z), tp: 4 (over y, core).
Axes of the slice: x: 2, y: 2, z: 4, core: 2. Of those that a mesh axis runs over, the one named last changes fastest.
Arguments:
- queries: bfloat16 [2, 512, 8192], P('pp', 'cp', 'tp'), may hold values from -9 to 9
- key_vectors: bfloat16 [2, 512, 512], P('pp', 'cp', 'tp'), may hold values from -6 to 6
- value_vectors: bfloat16 [2, 512, 512], P('pp', 'cp', 'tp'), may hold values from -30 to 30
- block_order: int32 [8], replicated, may hold values from 0 to 7, each once
- norm_gain: bfloat16 [2, 8192], P('pp', 'tp'), may hold values from 0.099609375 to 1.8984375
- kv_weight: bfloat16 [2, 8192, 1024], P('pp', 'tp'), may hold values from -0.0625 to 0.0625
Outputs:
- max_logits: float32 [2, 64], P('pp', 'tp')
- kv_next: bfloat16 [2, 512, 1024], P('pp', 'cp', 'tp')
Inputs may be any that keep to these rules, and one draw needn't show every extreme that they name: A permutation; rows 2 c * 64 to (2 c + 2) * 64 - 1 hold the positions of blocks block_order[2 c] and block_order[2 c + 1], in that order.
All inputs are finite; a program needn't handle non-finite values.
Results may differ from a plain program's by a relative error of at most 0.018.
Values may be sent and summed in bfloat16 or wider, within the bound.
No kernel may reach another device: no remote copies, remote signals or barrier semaphores. Data moves between devices by JAX's collectives and lax.ppermute only.
A program may use at most 128 MiB of HBM per device.

v0:
```python
import functools
import math

import jax
import jax.numpy as jnp
from jax import lax
from jax.experimental import pallas as pl
from jax.experimental.pallas import tpu as pltpu
from jax.sharding import PartitionSpec as P

DH = 128
CHUNKS = 2
SQUARE_ROWS = 16
MASKED = -1e30
LOG2E = math.log2(math.e)
F32 = jnp.float32
BF16 = jnp.bfloat16
WHOLE = pl.BlockSpec(memory_space=pltpu.VMEM)
SCALARS = pl.BlockSpec(memory_space=pltpu.SMEM)


def call(kernel, outs, args, specs=None, scratch=(), limit=16, name=None, aliases=None, micros=0):
    return pl.pallas_call(
        kernel,
        out_shape=outs,
        in_specs=specs or [WHOLE] * len(args),
        out_specs=jax.tree.map(lambda _: WHOLE, outs),
        scratch_shapes=scratch,
        name=name,
        input_output_aliases=aliases or {},
        cost_estimate=pl.CostEstimate(flops=int(micros * 1e9), bytes_accessed=0, transcendentals=0) if micros else None,
        compiler_params=pltpu.CompilerParams(vmem_limit_bytes=limit * 2**20),
    )(*args)


def bind_kernel(block_ref, *refs):
    refs[-1][...] = block_ref[...]


def bind(block, *after):
    return call(
        bind_kernel,
        jax.ShapeDtypeStruct(block.shape, block.dtype),
        (block, *after),
        [WHOLE] + [pl.BlockSpec(memory_space=pl.ANY)] * len(after),
        name="bind",
    )


def split(q_ref, after, *part_refs):
    width = part_refs[0].shape[1]
    for c, ref in enumerate(part_refs):
        ref[...] = q_ref[0, :, c * width:(c + 1) * width]


def prepare(order_ref, after, bias_ref):
    sources = lax.axis_size("cp")
    me = lax.axis_index("cp")
    rows = bias_ref.shape[1]
    block = rows // 2
    lane = lax.broadcasted_iota(jnp.int32, (1, rows), 1)
    q_block = jnp.where(lane < block, order_ref[2 * me], order_ref[2 * me + 1])
    q_pos = q_block * block + lax.rem(lane, block)
    for d in range(sources):
        source = lax.rem(me - d + sources, sources)
        for half in range(2):
            first = d * rows + half * block
            k_pos = order_ref[2 * source + half] * block + lax.broadcasted_iota(jnp.int32, (block, 1), 0)
            bias_ref[first:first + block, :] = jnp.where(k_pos <= q_pos, 0.0, MASKED)


def attend(first_head, heads, sources, q_ref, gain_ref, bias_ref, *refs):
    pairs = refs[:sources]
    before, (scaled_ref, square_ref, peak_ref, k_all, vt) = refs[sources:-5], refs[-5:]
    rows, width = q_ref.shape
    kv_local = pairs[0].shape[2] // DH
    factor = LOG2E / math.sqrt(DH)
    squares = jnp.zeros((1, rows), F32)
    if before:
        square_in, peak_in = before
        squares = square_in[:1, :]
        peak_ref[:, :first_head] = peak_in[...]
    for d in range(sources):
        part = slice(d * rows, (d + 1) * rows)
        k_all[part, :] = pairs[d][0]
        vt[:, part] = pairs[d][1].astype(F32).T.astype(BF16)
    bias = bias_ref[...]
    for i in range(0, width // DH, 2):
        h = first_head + i
        g = h // (heads // kv_local)
        group = slice(g * DH, (g + 1) * DH)
        q = jnp.concatenate([q_ref[:, i * DH:(i + 1) * DH], q_ref[:, (i + 1) * DH:(i + 2) * DH]], axis=0)
        s = lax.dot_general(k_all[:, group], q, (((1,), (1,)), ((), ())), preferred_element_type=F32)
        s = s * factor + jnp.concatenate([bias, bias], axis=1)
        m = jnp.max(s, axis=0, keepdims=True)
        p = jnp.exp2(s - m)
        total = jnp.sum(p, axis=0, keepdims=True)
        o = jnp.dot(vt[group, :], p.astype(BF16), preferred_element_type=F32)
        o = (o * (1.0 / total)).astype(BF16).astype(F32)
        for j in range(2):
            cols = slice((i + j) * DH, (i + j + 1) * DH)
            lanes = slice(j * rows, (j + 1) * rows)
            one = o[:, lanes]
            squares = squares + jnp.sum(one * one, axis=0, keepdims=True)
            gain = gain_ref[:, (h + j) * DH:(h + j + 1) * DH].astype(F32)
            scaled_ref[:, cols] = (one.T * gain).astype(BF16)
            peak_ref[:, h + j:h + j + 1] = jnp.max(m[:, lanes], axis=1, keepdims=True) * (1.0 / LOG2E)
    square_ref[...] = jnp.broadcast_to(squares, square_ref.shape)


def project(w_ref, square_ref, *refs):
    scaled, (give_ref, keep_ref) = refs[:-2], refs[-2:]
    rows, width = scaled[0].shape
    lanes = jnp.broadcast_to(square_ref[:1, :], (SQUARE_ROWS, rows))
    first = lanes.astype(BF16)
    rest = (lanes - first.astype(F32)).astype(BF16)
    groups, cols = give_ref.shape[0], give_ref.shape[2]
    core = lax.rem(lax.axis_index("tp"), 2)
    for ref, side in ((give_ref, 1 - core), (keep_ref, core)):
        for y in range(groups):
            at = pl.ds(pl.multiple_of((2 * y + side) * cols, cols), cols)
            part = jnp.dot(scaled[0][...], w_ref[:width, at], preferred_element_type=F32)
            for c in range(1, len(scaled)):
                part += jnp.dot(scaled[c][...], w_ref[c * width:(c + 1) * width, at], preferred_element_type=F32)
            ref[y, :rows, :] = part.astype(BF16)
            ref[y, rows:, :rows] = first
            ref[y, rows:, rows:2 * rows] = rest
            if cols > 2 * rows:
                ref[y, rows:, 2 * rows:] = jnp.zeros((SQUARE_ROWS, cols - 2 * rows), BF16)


def merge(keep_ref, got_ref, peak_ref, peak_got, peak_out, *give_refs):
    groups = keep_ref.shape[0]
    mine = lax.axis_index("tp") // 2
    peak_out[...] = jnp.maximum(peak_ref[...], peak_got[...])
    for step, ref in enumerate(give_refs):
        y = lax.rem(mine + step, groups)
        total = keep_ref[y].astype(F32) + got_ref[y].astype(F32)
        ref[...] = total.astype(ref.dtype)


def finish(features, peak_ref, peak_got, keep_ref, *refs):
    peak_out, out_ref = refs[-2:]
    rows = out_ref.shape[0]
    peak_out[...] = jnp.maximum(peak_ref[...], peak_got[...])
    total = keep_ref[...]
    for ref in refs[:-2]:
        total = total + ref[...].astype(F32)
    squares = total[rows:rows + 8, :rows] + total[rows:rows + 8, rows:2 * rows]
    inverse = lax.rsqrt(squares / features + 1e-05)
    column = jnp.broadcast_to(inverse[:1, :], (rows, rows)).T[:, :1]
    out_ref[...] = (total[:rows, :] * column).astype(BF16)


def shifted(block, axis, distance):
    size = lax.axis_size(axis)
    return lax.ppermute(block, axis, [((i - distance) % size, i) for i in range(size)])


def partner(index, step, size):
    return (index + step) % size if size & (size - 1) else index ^ step


def swapped(block, axis, step):
    size = lax.axis_size(axis)
    return lax.ppermute(block, axis, [(i, partner(i, step, size)) for i in range(size)])


def returned(block, step):
    sections, sources = lax.axis_size("pp"), lax.axis_size("cp")
    route = [
        (s * sources + c, (s - 1) % sections * sources + partner(c, step, sources))
        for s in range(sections)
        for c in range(sources)
    ]
    return lax.ppermute(block, ("pp", "cp"), route)


def on_device(queries, key_vectors, value_vectors, block_order, norm_gain, kv_weight):
    rows, width = queries.shape[1:]
    heads = width // DH
    peers = lax.axis_size("tp")
    sources = lax.axis_size("cp")
    kv_width = key_vectors.shape[2]
    columns = kv_weight.shape[2]
    out_cols = columns // peers
    shape = jax.ShapeDtypeStruct
    steps = [2**i for i in range((sources - 1).bit_length())]

    pair_here = jnp.concatenate([key_vectors, value_vectors])
    pair = shifted(pair_here, "pp", 1)
    part_width = width // CHUNKS
    parts = call(
        split, [shape((rows, part_width), BF16)] * CHUNKS, (queries, pair_here), [WHOLE, pl.BlockSpec(memory_space=pl.ANY)], name="split"
    )
    parts = [shifted(part, "pp", 1) for part in parts]
    pairs = [pair] + [shifted(pair, "cp", d) for d in range(1, sources)]
    bias = call(
        prepare,
        shape((sources * rows, rows), F32),
        (block_order, pair),
        [SCALARS, pl.BlockSpec(memory_space=pl.ANY)],
        name="prepare",
        micros=4,
    )
    scaled, before = [], ()
    for c in range(CHUNKS):
        first = c * part_width // DH
        part, *before = call(
            functools.partial(attend, first, heads, sources),
            (
                shape((rows, part_width), BF16),
                shape((8, rows), F32),
                shape((1, first + part_width // DH), F32),
            ),
            (parts[c], norm_gain, bias, *pairs, *before),
            scratch=[pltpu.VMEM((sources * rows, kv_width), BF16), pltpu.VMEM((kv_width, sources * rows), BF16)],
            name="attend",
            micros=1.5,
        )
        scaled.append(part)
    squares, peak = before
    slab = shape((peers // 2, rows + SQUARE_ROWS, out_cols), BF16)
    give, keep = call(project, (slab, slab), (kv_weight[0], squares, *scaled), name="project", micros=1)
    peak = bind(peak, give)
    got = lax.ppermute(give, "tp", [(i, i ^ 1) for i in range(peers)])
    slab = (rows + SQUARE_ROWS, out_cols)
    peak, mine, *others = call(
        merge,
        [shape((1, heads), F32), shape(slab, F32)] + [shape(slab, BF16)] * (peers // 2 - 1),
        (keep, got, shifted(peak, "pp", -1), returned(peak, steps[0])),
        name="merge",
    )
    for step in steps[1:-1]:
        peak = jnp.maximum(peak, swapped(peak, "cp", step))
    others = [
        lax.ppermute(block, "tp", [(i, (i + 2 * (step + 1)) % peers) for i in range(peers)])
        for step, block in enumerate(others)
    ]
    max_logits, kv_next = call(
        functools.partial(finish, width * peers),
        (shape((1, heads), F32), shape((rows, out_cols), BF16)),
        (peak, swapped(peak, "cp", steps[-1]), mine, *others),
        name="finish",
    )
    return (max_logits, kv_next[None])


def solution(mesh):
    return jax.shard_map(
        on_device,
        mesh=mesh,
        in_specs=(
            P("pp", "cp", "tp"),
            P("pp", "cp", "tp"),
            P("pp", "cp", "tp"),
            P(),
            P("pp", "tp"),
            P("pp", "tp", None),
        ),
        out_specs=(P("pp", "tp"), P("pp", "cp", "tp")),
        check_vma=False,
    )
```

profile of v0, /device:TPU:0, one launch (start us, length us, event | category | flops | bytes accessed | tf_op | source)
XLA Modules:
  0.0 36.8 jit_solution(5342151891539784872)
XLA Ops:
  0.6 0.8 %constant_dynamic-update-slice_fusion.1 = bf16[2,128,128]{2,1,0:T(8,128)(2,1)S(1)} fusion(bf16[1,128,128]{2,1,0:T(8,128)(2,1)} %param.7), kind=kLoop, calls=%fused_computation.1 | loop fusion | bytes 65536
  1.4 0.8 %constant_dynamic-update-slice_fusion.after = bf16[2,128,128]{2,1,0:T(8,128)(2,1)S(1)} fusion(bf16[2,128,128]{2,1,0:T(8,128)(2,1)S(1)} %constant_dynamic-update-slice_fusion.1, bf16[1,128,128]{2,1,0:T(8,128)(2,1)} %param.8), kind=kLoop, calls=%fused_computation | loop fusion | bytes 65536 | tf_op jit(solution)/shard_map/concatenate | solution.py:190
  2.2 2.9 %collective-permute-start.1 = (bf16[2,128,128]{2,1,0:T(8,128)(2,1)S(1)}, bf16[2,128,128]{2,1,0:T(8,128)(2,1)S(1)}, u32[]{:S(2)}, u32[]{:S(2)}) collective-permute-start(bf16[2,128,128]{2,1,0:T(8,128)(2,1)S(1)} %constant_dynamic-update-slice_fusion.after), channel_id=1, source_target_pairs={{16,0},{0,16},{17,1},{1,17},{18,2},{2,18},{19,3},{3,19},{20,4},{4,... | collective-permute-start | bytes 196616 | tf_op jit(solution)/shard_map/ppermute | solution.py:157
  5.1 1.0 %copy-done.1 = bf16[1,128,2048]{2,1,0:T(8,128)(2,1)S(1)} copy-done((bf16[1,128,2048]{2,1,0:T(8,128)(2,1)S(1)}, bf16[1,128,2048]{2,1,0:T(8,128)(2,1)}, u32[]{:S(2)}) %copy-start.1) | copy-done | bytes 524312
  6.2 0.1 collective-permute-start
  6.3 2.0 %collective-permute-start.5 = (bf16[128,1024]{1,0:T(8,128)(2,1)S(1)}, bf16[128,1024]{1,0:T(8,128)(2,1)S(1)}, u32[]{:S(2)}, u32[]{:S(2)}) collective-permute-start(bf16[128,1024]{1,0:T(8,128)(2,1)S(1)} %get-tuple-element.18), channel_id=1, source_target_pairs={{16,0},{0,16},{17,1},{1,17},{18,2},{2,18},{19,3},{3,19},{20,4},{4,... | collective-permute-start | bytes 786440 | tf_op jit(solution)/shard_map/ppermute | solution.py:157
  8.3 3.6 %collective-permute-start.4 = (bf16[2,128,128]{2,1,0:T(8,128)(2,1)S(1)}, bf16[2,128,128]{2,1,0:T(8,128)(2,1)S(1)}, u32[]{:S(2)}, u32[]{:S(2)}) collective-permute-start(bf16[2,128,128]{2,1,0:T(8,128)(2,1)S(1)} %collective-permute-done.1.after.refs_0_), channel_id=1, source_target_pairs={{4,0},{8,4},{12,8},{0,12},{5,1},{9,5},{13,9},{1,13},{6,2},{10,6},{... | collective-permute-start | bytes 196616 | tf_op jit(solution)/shard_map/ppermute | solution.py:157
  11.9 1.0 %collective-permute-start.2 = (bf16[2,128,128]{2,1,0:T(8,128)(2,1)S(1)}, bf16[2,128,128]{2,1,0:T(8,128)(2,1)S(1)}, u32[]{:S(2)}, u32[]{:S(2)}) collective-permute-start(bf16[2,128,128]{2,1,0:T(8,128)(2,1)S(1)} %collective-permute-done.1.after.refs_0_), channel_id=1, source_target_pairs={{12,0},{0,4},{4,8},{8,12},{13,1},{1,5},{5,9},{9,13},{14,2},{2,6},{... | collective-permute-start | bytes 196616 | tf_op jit(solution)/shard_map/ppermute | solution.py:157
  12.9 0.7 %copy-done.3 = s32[8]{0:T(128)S(1)} copy-done((s32[8]{0:T(128)S(1)}, s32[8]{0:T(128)}, u32[]{:S(2)}) %copy-start.3) | copy-done | bytes 56
  13.5 0.6 %prepare.1.bias_ref = f32[512,128]{1,0:T(8,128)S(1)} custom-call(s32[8]{0:T(128)S(1)} %copy-done.3, bf16[2,128,128]{2,1,0:T(8,128)(2,1)S(1)} %collective-permute-done.1.after.refs_0_), custom_call_target="tpu_custom_call" | custom-call | flops 4000000000 | tf_op jit(solution)/shard_map/prepare/pallas_call | solution.py:23
  14.2 2.9 %collective-permute-done.3.refs_2_ = bf16[2,128,128]{2,1,0:T(8,128)(2,1)S(1)} collective-permute-done((bf16[2,128,128]{2,1,0:T(8,128)(2,1)S(1)}, bf16[2,128,128]{2,1,0:T(8,128)(2,1)S(1)}, u32[]{:S(2)}, u32[]{:S(2)}) %collective-permute-start.3) | collective-permute-done | bytes 65568 | tf_op jit(solution)/shard_map/ppermute | solution.py:157
  17.0 0.9 %collective-permute-done.2.refs_1_ = bf16[2,128,128]{2,1,0:T(8,128)(2,1)S(1)} collective-permute-done((bf16[2,128,128]{2,1,0:T(8,128)(2,1)S(1)}, bf16[2,128,128]{2,1,0:T(8,128)(2,1)S(1)}, u32[]{:S(2)}, u32[]{:S(2)}) %collective-permute-start.2) | collective-permute-done | bytes 65568 | tf_op jit(solution)/shard_map/ppermute | solution.py:157
  17.9 1.7 %collective-permute-done.5.q_ref = bf16[128,1024]{1,0:T(8,128)(2,1)S(1)} collective-permute-done((bf16[128,1024]{1,0:T(8,128)(2,1)S(1)}, bf16[128,1024]{1,0:T(8,128)(2,1)S(1)}, u32[]{:S(2)}, u32[]{:S(2)}) %collective-permute-start.5) | collective-permute-done | bytes 262176 | tf_op jit(solution)/shard_map/ppermute | solution.py:157
  19.6 1.9 %attend.2 = (bf16[128,1024]{1,0:T(8,128)(2,1)S(1)}, f32[8,128]{1,0:T(8,128)S(1)}, f32[1,8]{1,0:T(1,128)S(1)}) custom-call(bf16[128,1024]{1,0:T(8,128)(2,1)S(1)} %collective-permute-done.5.q_ref, bf16[1,2048]{1,0:T(2,128)(2,1)S(1)} %copy-done.2, f32[512,128]{1,0:T(8,128)S(1)} %prepare.1.bias_ref, ...), custom_call_target="tpu_custom_call" | custom-call | flops 1500000000 | tf_op jit(solution)/shard_map/attend/pallas_call | solution.py:23
  21.5 1.9 %attend.3 = (bf16[128,1024]{1,0:T(8,128)(2,1)S(1)}, f32[8,128]{1,0:T(8,128)S(1)}, f32[1,16]{1,0:T(1,128)S(1)}) custom-call(bf16[128,1024]{1,0:T(8,128)(2,1)S(1)} %collective-permute-done.q_ref, bf16[1,2048]{1,0:T(2,128)(2,1)S(1)} %copy-done.2, f32[512,128]{1,0:T(8,128)S(1)} %prepare.1.bias_ref, ...), custom_call_target="tpu_custom_call" | custom-call | flops 1500000000 | tf_op jit(solution)/shard_map/attend/pallas_call | solution.py:23
  23.4 0.8 %project.1 = (bf16[2,144,256]{2,1,0:T(8,128)(2,1)S(1)}, bf16[2,144,256]{2,1,0:T(8,128)(2,1)S(1)}) custom-call(bf16[2048,1024]{1,0:T(8,128)(2,1)S(1)} %bitcast.2, f32[8,128]{1,0:T(8,128)S(1)} %get-tuple-element.21.square_ref, bf16[128,1024]{1,0:T(8,128)(2,1)S(1)} %get-tuple-element.22.refs_0_, bf16[128,1024]{1,0:T(8,128)(2,1)S(1)} %get-tuple-element.23.refs_1_), custom_call_target="tpu_custom_call" | custom-call | flops 1000000000 | tf_op jit(solution)/shard_map/project/pallas_call | solution.py:23
  24.3 2.0 %collective-permute-start.8 = (f32[1,16]{1,0:T(1,128)S(1)}, f32[1,16]{1,0:T(1,128)S(1)}, u32[]{:S(2)}, u32[]{:S(2)}) collective-permute-start(f32[1,16]{1,0:T(1,128)S(1)} %bind.1), channel_id=1, source_target_pairs={{0,20},{4,16},{8,28},{12,24},{16,4},{20,0},{24,12},{28,8},{1,21},{... | collective-permute-start | bytes 200 | tf_op jit(solution)/shard_map/ppermute | solution.py:176
  26.4 1.1 %collective-permute-start.7 = (f32[1,16]{1,0:T(1,128)S(1)}, f32[1,16]{1,0:T(1,128)S(1)}, u32[]{:S(2)}, u32[]{:S(2)}) collective-permute-start(f32[1,16]{1,0:T(1,128)S(1)} %bind.1), channel_id=1, source_target_pairs={{16,0},{0,16},{17,1},{1,17},{18,2},{2,18},{19,3},{3,19},{20,4},{4,... | collective-permute-start | bytes 200 | tf_op jit(solution)/shard_map/ppermute | solution.py:157
  27.4 1.4 %collective-permute-done.8.peak_got = f32[1,16]{1,0:T(1,128)S(1)} collective-permute-done((f32[1,16]{1,0:T(1,128)S(1)}, f32[1,16]{1,0:T(1,128)S(1)}, u32[]{:S(2)}, u32[]{:S(2)}) %collective-permute-start.8) | collective-permute-done | bytes 96 | tf_op jit(solution)/shard_map/ppermute | solution.py:176
  28.8 1.1 %collective-permute-done.7.peak_ref = f32[1,16]{1,0:T(1,128)S(1)} collective-permute-done((f32[1,16]{1,0:T(1,128)S(1)}, f32[1,16]{1,0:T(1,128)S(1)}, u32[]{:S(2)}, u32[]{:S(2)}) %collective-permute-start.7) | collective-permute-done | bytes 96 | tf_op jit(solution)/shard_map/ppermute | solution.py:157
  29.9 1.6 %collective-permute-start.10 = (bf16[144,256]{1,0:T(8,128)(2,1)S(1)}, bf16[144,256]{1,0:T(8,128)(2,1)S(1)}, u32[]{:S(2)}, u32[]{:S(2)}) collective-permute-start(bf16[144,256]{1,0:T(8,128)(2,1)S(1)} %get-tuple-element.29), channel_id=1, source_target_pairs={{0,2},{1,3},{2,0},{3,1},{4,6},{5,7},{6,4},{7,5},{8,10},{9,11},{10,... | collective-permute-start | bytes 221192 | tf_op jit(solution)/shard_map/ppermute | solution.py:237
  31.5 2.6 %collective-permute-start.9 = (f32[1,16]{1,0:T(1,128)S(1)}, f32[1,16]{1,0:T(1,128)S(1)}, u32[]{:S(2)}, u32[]{:S(2)}) collective-permute-start(f32[1,16]{1,0:T(1,128)S(1)} %get-tuple-element.27.peak_ref), channel_id=1, source_target_pairs={{0,8},{4,12},{8,0},{12,4},{1,9},{5,13},{9,1},{13,5},{2,10},{6,14},... | collective-permute-start | bytes 200 | tf_op jit(solution)/shard_map/ppermute | solution.py:166
  34.1 1.8 %collective-permute-done.9.peak_got = f32[1,16]{1,0:T(1,128)S(1)} collective-permute-done((f32[1,16]{1,0:T(1,128)S(1)}, f32[1,16]{1,0:T(1,128)S(1)}, u32[]{:S(2)}, u32[]{:S(2)}) %collective-permute-start.9) | collective-permute-done | bytes 96 | tf_op jit(solution)/shard_map/ppermute | solution.py:166
  36.0 0.8 %finish.1 = (f32[1,16]{1,0:T(1,128)}, bf16[128,256]{1,0:T(8,128)(2,1)}) custom-call(f32[1,16]{1,0:T(1,128)S(1)} %get-tuple-element.27.peak_ref, f32[1,16]{1,0:T(1,128)S(1)} %collective-permute-done.9.peak_got, f32[144,256]{1,0:T(8,128)S(1)} %get-tuple-element.28.keep_ref, bf16[144,256]{1,0:T(8,128)(2,1)S(1)} %collective-permute-done.10.refs_0_), custom_call_target="tpu_custom_call" | custom-call | tf_op jit(solution)/shard_map/finish/pallas_call | solution.py:23
  (16 shorter events, 0.2 us)
Async XLA Ops:
  2.2 6.1 %collective-permute-start.1 = (bf16[2,128,128]{2,1,0:T(8,128)(2,1)S(1)}, bf16[2,128,128]{2,1,0:T(8,128)(2,1)S(1)}, u32[]{:S(2)}, u32[]{:S(2)}) collective-permute-start(bf16[2,128,128]{2,1,0:T(8,128)(2,1)S(1)} %constant_dynamic-update-slice_fusion.after), channel_id=1, source_target_pairs={{16,0},{0,16},{17,1},{1,17},{18,2},{2,18},{19,3},{3,19},{20,4},{4,... | collective-permute-start | bytes 196616 | tf_op jit(solution)/shard_map/ppermute | solution.py:157
  5.1 1.0 %copy-start.1 = (bf16[1,128,2048]{2,1,0:T(8,128)(2,1)S(1)}, bf16[1,128,2048]{2,1,0:T(8,128)(2,1)}, u32[]{:S(2)}) copy-start(bf16[1,128,2048]{2,1,0:T(8,128)(2,1)} %q_ref.1) | copy-start | bytes 1572868
  6.2 15.3 %collective-permute-start = (bf16[128,1024]{1,0:T(8,128)(2,1)S(1)}, bf16[128,1024]{1,0:T(8,128)(2,1)S(1)}, u32[]{:S(2)}, u32[]{:S(2)}) collective-permute-start(bf16[128,1024]{1,0:T(8,128)(2,1)S(1)} %get-tuple-element.17), channel_id=1, source_target_pairs={{16,0},{0,16},{17,1},{1,17},{18,2},{2,18},{19,3},{3,19},{20,4},{4,... | collective-permute-start | bytes 786440 | tf_op jit(solution)/shard_map/ppermute | solution.py:157
  6.3 13.4 %copy-start.2 = (bf16[1,2048]{1,0:T(2,128)(2,1)S(1)}, bf16[1,2048]{1,0:T(2,128)(2,1)}, u32[]{:S(2)}) copy-start(bf16[1,2048]{1,0:T(2,128)(2,1)} %gain_ref.3) | copy-start | bytes 12292
  6.3 13.4 %collective-permute-start.5 = (bf16[128,1024]{1,0:T(8,128)(2,1)S(1)}, bf16[128,1024]{1,0:T(8,128)(2,1)S(1)}, u32[]{:S(2)}, u32[]{:S(2)}) collective-permute-start(bf16[128,1024]{1,0:T(8,128)(2,1)S(1)} %get-tuple-element.18), channel_id=1, source_target_pairs={{16,0},{0,16},{17,1},{1,17},{18,2},{2,18},{19,3},{3,19},{20,4},{4,... | collective-permute-start | bytes 786440 | tf_op jit(solution)/shard_map/ppermute | solution.py:157
  8.3 5.9 %collective-permute-start.4 = (bf16[2,128,128]{2,1,0:T(8,128)(2,1)S(1)}, bf16[2,128,128]{2,1,0:T(8,128)(2,1)S(1)}, u32[]{:S(2)}, u32[]{:S(2)}) collective-permute-start(bf16[2,128,128]{2,1,0:T(8,128)(2,1)S(1)} %collective-permute-done.1.after.refs_0_), channel_id=1, source_target_pairs={{4,0},{8,4},{12,8},{0,12},{5,1},{9,5},{13,9},{1,13},{6,2},{10,6},{... | collective-permute-start | bytes 196616 | tf_op jit(solution)/shard_map/ppermute | solution.py:157
  11.9 5.2 %collective-permute-start.3 = (bf16[2,128,128]{2,1,0:T(8,128)(2,1)S(1)}, bf16[2,128,128]{2,1,0:T(8,128)(2,1)S(1)}, u32[]{:S(2)}, u32[]{:S(2)}) collective-permute-start(bf16[2,128,128]{2,1,0:T(8,128)(2,1)S(1)} %collective-permute-done.1.after.refs_0_), channel_id=1, source_target_pairs={{8,0},{12,4},{0,8},{4,12},{9,1},{13,5},{1,9},{5,13},{10,2},{14,6},... | collective-permute-start | bytes 196616 | tf_op jit(solution)/shard_map/ppermute | solution.py:157
  11.9 6.1 %collective-permute-start.2 = (bf16[2,128,128]{2,1,0:T(8,128)(2,1)S(1)}, bf16[2,128,128]{2,1,0:T(8,128)(2,1)S(1)}, u32[]{:S(2)}, u32[]{:S(2)}) collective-permute-start(bf16[2,128,128]{2,1,0:T(8,128)(2,1)S(1)} %collective-permute-done.1.after.refs_0_), channel_id=1, source_target_pairs={{12,0},{0,4},{4,8},{8,12},{13,1},{1,5},{5,9},{9,13},{14,2},{2,6},{... | collective-permute-start | bytes 196616 | tf_op jit(solution)/shard_map/ppermute | solution.py:157
  12.9 0.7 %copy-start.3 = (s32[8]{0:T(128)S(1)}, s32[8]{0:T(128)}, u32[]{:S(2)}) copy-start(s32[8]{0:T(128)} %order_ref.1) | copy-start | bytes 100
  14.1 9.3 %copy-start = (bf16[1,2048,1024]{2,1,0:T(8,128)(2,1)S(1)}, bf16[1,2048,1024]{2,1,0:T(8,128)(2,1)}, u32[]{:S(2)}) copy-start(bf16[1,2048,1024]{2,1,0:T(8,128)(2,1)} %param.11) | copy-start | bytes 12582916
  24.2 5.7 %collective-permute-start.6 = (bf16[2,144,256]{2,1,0:T(8,128)(2,1)S(1)}, bf16[2,144,256]{2,1,0:T(8,128)(2,1)S(1)}, u32[]{:S(2)}, u32[]{:S(2)}) collective-permute-start(bf16[2,144,256]{2,1,0:T(8,128)(2,1)S(1)} %get-tuple-element.25.refs_0_), channel_id=1, source_target_pairs={{0,1},{1,0},{2,3},{3,2},{4,5},{5,4},{6,7},{7,6},{8,9},{9,8},{10,11... | collective-permute-start | bytes 442376 | tf_op jit(solution)/shard_map/ppermute | solution.py:226
  24.3 4.5 %collective-permute-start.8 = (f32[1,16]{1,0:T(1,128)S(1)}, f32[1,16]{1,0:T(1,128)S(1)}, u32[]{:S(2)}, u32[]{:S(2)}) collective-permute-start(f32[1,16]{1,0:T(1,128)S(1)} %bind.1), channel_id=1, source_target_pairs={{0,20},{4,16},{8,28},{12,24},{16,4},{20,0},{24,12},{28,8},{1,21},{... | collective-permute-start | bytes 200 | tf_op jit(solution)/shard_map/ppermute | solution.py:176
  26.4 3.5 %collective-permute-start.7 = (f32[1,16]{1,0:T(1,128)S(1)}, f32[1,16]{1,0:T(1,128)S(1)}, u32[]{:S(2)}, u32[]{:S(2)}) collective-permute-start(f32[1,16]{1,0:T(1,128)S(1)} %bind.1), channel_id=1, source_target_pairs={{16,0},{0,16},{17,1},{1,17},{18,2},{2,18},{19,3},{3,19},{20,4},{4,... | collective-permute-start | bytes 200 | tf_op jit(solution)/shard_map/ppermute | solution.py:157
  29.9 6.0 %collective-permute-start.10 = (bf16[144,256]{1,0:T(8,128)(2,1)S(1)}, bf16[144,256]{1,0:T(8,128)(2,1)S(1)}, u32[]{:S(2)}, u32[]{:S(2)}) collective-permute-start(bf16[144,256]{1,0:T(8,128)(2,1)S(1)} %get-tuple-element.29), channel_id=1, source_target_pairs={{0,2},{1,3},{2,0},{3,1},{4,6},{5,7},{6,4},{7,5},{8,10},{9,11},{10,... | collective-permute-start | bytes 221192 | tf_op jit(solution)/shard_map/ppermute | solution.py:237
  31.5 4.4 %collective-permute-start.9 = (f32[1,16]{1,0:T(1,128)S(1)}, f32[1,16]{1,0:T(1,128)S(1)}, u32[]{:S(2)}, u32[]{:S(2)}) collective-permute-start(f32[1,16]{1,0:T(1,128)S(1)} %get-tuple-element.27.peak_ref), channel_id=1, source_target_pairs={{0,8},{4,12},{8,0},{12,4},{1,9},{5,13},{9,1},{13,5},{2,10},{6,14},... | collective-permute-start | bytes 200 | tf_op jit(solution)/shard_map/ppermute | solution.py:166
where the time goes:
time: 37.1 us; the launch traced here: 36.8 us
  starting transfers between devices  17 us (46%)
  waiting for transfers between devices  9.8 us (26%)
  Pallas kernels  6.03 us (16%)
  local copies, waits for them, and re-layouts  3.24 us (9%)
  between operations  0.74 us (2%)
    ppermute x7, starting transfers between devices, shifted(): lax.ppermute(block, axis, [((i - distance) % size, i) for i in range(size)])  10.7 us
    ppermute x7, waiting for transfers between devices, shifted(): lax.ppermute(block, axis, [((i - distance) % size, i) for i in range(size)])  6.55 us
    pallas_call x8, Pallas kernels, call(): pl.pallas_call(kernel, out_shape=outs, in_specs=specs or [WHOLE] * len(ar...  6.03 us
    ppermute x1, starting transfers between devices, swapped(): lax.ppermute(block, axis, [(i, partner(i, step, size)) for i in range(siz...  2.59 us
    unnamed x9, local copies, waits for them, and re-layouts  2.47 us
    ppermute x1, starting transfers between devices, returned(): return lax.ppermute(block, ('pp', 'cp'), route)  2.05 us
    ppermute x1, waiting for transfers between devices, swapped(): lax.ppermute(block, axis, [(i, partner(i, step, size)) for i in range(siz...  1.85 us
    ppermute x1, starting transfers between devices, on_device(): lax.ppermute(block, 'tp', [(i, (i + 2 * (step + 1)) % peers) for i in ran...  1.58 us
  transfers between devices with their start and end apart: 11, of which 6 were waited for; matrix products, arithmetic and copies ran while one was open for 0% of the time, Pallas kernels for 7%

commit v1 on v0

--- a/solution.py
+++ b/solution.py
@@ -9,9 +9,9 @@
 from jax.sharding import PartitionSpec as P
 
 DH = 128
-CHUNKS = 2
+LANES = 128
 SQUARE_ROWS = 16
-MASKED = -1e30
+MASKED = -(2.0**100)
 LOG2E = math.log2(math.e)
 F32 = jnp.float32
 BF16 = jnp.bfloat16
@@ -47,70 +47,78 @@
     )
 
 
-def split(q_ref, after, *part_refs):
-    width = part_refs[0].shape[1]
-    for c, ref in enumerate(part_refs):
-        ref[...] = q_ref[0, :, c * width:(c + 1) * width]
-
-
-def prepare(order_ref, after, bias_ref):
+def prepare(order_ref, after, feature_ref):
     sources = lax.axis_size("cp")
     me = lax.axis_index("cp")
-    rows = bias_ref.shape[1]
+    block = feature_ref.shape[1] // (2 * sources)
+    row = lax.broadcasted_iota(jnp.int32, (block, LANES), 0)
+    lane = lax.broadcasted_iota(jnp.int32, (block, LANES), 1)
+    for side in range(2):
+        mine = order_ref[2 * me + side]
+        for d in range(sources):
+            source = lax.rem(me - d + sources, sources)
+            for half in range(2):
+                other = order_ref[2 * source + half]
+                column = jnp.where(other == mine, row, jnp.where(other > mine, block, -1))
+                first = (2 * d + half) * block
+                feature_ref[side, first:first + block, :] = jnp.where(lane == column, 1.0, 0.0).astype(BF16)
+
+
+def attend(sources, q_ref, gain_ref, feature_ref, *refs):
+    pairs = refs[:sources]
+    scaled_ref, square_ref, peak_ref, k_all, vt = refs[sources:]
+    rows, width = q_ref.shape[1:]
     block = rows // 2
-    lane = lax.broadcasted_iota(jnp.int32, (1, rows), 1)
-    q_block = jnp.where(lane < block, order_ref[2 * me], order_ref[2 * me + 1])
-    q_pos = q_block * block + lax.rem(lane, block)
-    for d in range(sources):
-        source = lax.rem(me - d + sources, sources)
-        for half in range(2):
-            first = d * rows + half * block
-            k_pos = order_ref[2 * source + half] * block + lax.broadcasted_iota(jnp.int32, (block, 1), 0)
-            bias_ref[first:first + block, :] = jnp.where(k_pos <= q_pos, 0.0, MASKED)
-
-
-def attend(first_head, heads, sources, q_ref, gain_ref, bias_ref, *refs):
-    pairs = refs[:sources]
-    before, (scaled_ref, square_ref, peak_ref, k_all, vt) = refs[sources:-5], refs[-5:]
-    rows, width = q_ref.shape
+    heads = width // DH
     kv_local = pairs[0].shape[2] // DH
-    factor = LOG2E / math.sqrt(DH)
-    squares = jnp.zeros((1, rows), F32)
-    if before:
-        square_in, peak_in = before
-        squares = square_in[:1, :]
-        peak_ref[:, :first_head] = peak_in[...]
-    for d in range(sources):
-        part = slice(d * rows, (d + 1) * rows)
-        k_all[part, :] = pairs[d][0]
-        vt[:, part] = pairs[d][1].astype(F32).T.astype(BF16)
-    bias = bias_ref[...]
-    for i in range(0, width // DH, 2):
-        h = first_head + i
-        g = h // (heads // kv_local)
+    tile = 256 // block
+    scale = 1.0 / math.sqrt(DH)
+    ahead = lax.rem(lax.broadcasted_iota(jnp.int32, (tile * block, LANES), 0), block)
+    lane = lax.broadcasted_iota(jnp.int32, (tile * block, LANES), 1)
+    blocked = jnp.where((lane > ahead) & (lane <= block), MASKED, 0.0).astype(BF16)
+    squares = [jnp.zeros((1, tile * block), F32)] * 2
+    vt[DH:, :] = jnp.ones((vt.shape[0] - DH, vt.shape[1]), BF16)
+    for side in range(2):
+        k_all[side, :, DH:] = feature_ref[side]
+    for g in range(kv_local):
         group = slice(g * DH, (g + 1) * DH)
-        q = jnp.concatenate([q_ref[:, i * DH:(i + 1) * DH], q_ref[:, (i + 1) * DH:(i + 2) * DH]], axis=0)
-        s = lax.dot_general(k_all[:, group], q, (((1,), (1,)), ((), ())), preferred_element_type=F32)
-        s = s * factor + jnp.concatenate([bias, bias], axis=1)
-        m = jnp.max(s, axis=0, keepdims=True)
-        p = jnp.exp2(s - m)
-        total = jnp.sum(p, axis=0, keepdims=True)
-        o = jnp.dot(vt[group, :], p.astype(BF16), preferred_element_type=F32)
-        o = (o * (1.0 / total)).astype(BF16).astype(F32)
-        for j in range(2):
-            cols = slice((i + j) * DH, (i + j + 1) * DH)
-            lanes = slice(j * rows, (j + 1) * rows)
-            one = o[:, lanes]
-            squares = squares + jnp.sum(one * one, axis=0, keepdims=True)
-            gain = gain_ref[:, (h + j) * DH:(h + j + 1) * DH].astype(F32)
-            scaled_ref[:, cols] = (one.T * gain).astype(BF16)
-            peak_ref[:, h + j:h + j + 1] = jnp.max(m[:, lanes], axis=1, keepdims=True) * (1.0 / LOG2E)
-    square_ref[...] = jnp.broadcast_to(squares, square_ref.shape)
-
-
-def project(w_ref, square_ref, *refs):
-    scaled, (give_ref, keep_ref) = refs[:-2], refs[-2:]
-    rows, width = scaled[0].shape
+        for d in range(sources):
+            part = slice(d * rows, (d + 1) * rows)
+            for side in range(2):
+                k_all[side, part, :DH] = pairs[d][0, :, group]
+            vt[:DH, part] = pairs[d][1, :, group].astype(F32).T.astype(BF16)
+        for first in range(g * heads // kv_local, (g + 1) * heads // kv_local, tile):
+            peaks = []
+            for side in range(2):
+                tokens = slice(side * block, (side + 1) * block)
+                q = jnp.concatenate([q_ref[0, tokens, h * DH:(h + 1) * DH] for h in range(first, first + tile)], axis=0)
+                q = jnp.concatenate([q, blocked], axis=1)
+                s = lax.dot_general(k_all[side], q, (((1,), (1,)), ((), ())), preferred_element_type=F32)
+                m = jnp.max(s, axis=0, keepdims=True)
+                p = jnp.exp2((s - m) * (scale * LOG2E)).astype(BF16)
+                o = jnp.dot(vt[...], p, preferred_element_type=F32)
+                o = (o[:DH, :] * (1.0 / o[DH:DH + 1, :])).astype(BF16)
+                wide = o.astype(F32)
+                squares[side] = squares[side] + jnp.sum(wide * wide, axis=0, keepdims=True)
+                peaks.append(m)
+                turned = o.T.astype(F32)
+                for j in range(tile):
+                    cols = slice((first + j) * DH, (first + j + 1) * DH)
+                    one = turned[j * block:(j + 1) * block, :]
+                    scaled_ref[tokens, cols] = (one * gain_ref[:, cols].astype(F32)).astype(BF16)
+            peak = jnp.maximum(*peaks)
+            for j in range(tile):
+                one = jnp.max(peak[:, j * block:(j + 1) * block], axis=1, keepdims=True)
+                peak_ref[:, first + j:first + j + 1] = one * scale
+    for side in range(2):
+        total = squares[side][:, :block]
+        for j in range(1, tile):
+            total = total + squares[side][:, j * block:(j + 1) * block]
+        square_ref[:, side * block:(side + 1) * block] = jnp.broadcast_to(total, (8, block))
+
+
+def project(w_ref, square_ref, scaled_ref, give_ref, keep_ref):
+    rows = scaled_ref.shape[0]
     lanes = jnp.broadcast_to(square_ref[:1, :], (SQUARE_ROWS, rows))
     first = lanes.astype(BF16)
     rest = (lanes - first.astype(F32)).astype(BF16)
@@ -119,9 +127,7 @@
     for ref, side in ((give_ref, 1 - core), (keep_ref, core)):
         for y in range(groups):
             at = pl.ds(pl.multiple_of((2 * y + side) * cols, cols), cols)
-            part = jnp.dot(scaled[0][...], w_ref[:width, at], preferred_element_type=F32)
-            for c in range(1, len(scaled)):
-                part += jnp.dot(scaled[c][...], w_ref[c * width:(c + 1) * width, at], preferred_element_type=F32)
+            part = jnp.dot(scaled_ref[...], w_ref[:, at], preferred_element_type=F32)
             ref[y, :rows, :] = part.astype(BF16)
             ref[y, rows:, :rows] = first
             ref[y, rows:, rows:2 * rows] = rest
@@ -187,41 +193,29 @@
     shape = jax.ShapeDtypeStruct
     steps = [2**i for i in range((sources - 1).bit_length())]
 
-    pair_here = jnp.concatenate([key_vectors, value_vectors])
+    pair_here = jnp.stack([key_vectors[0], value_vectors[0]])
     pair = shifted(pair_here, "pp", 1)
-    part_width = width // CHUNKS
-    parts = call(
-        split, [shape((rows, part_width), BF16)] * CHUNKS, (queries, pair_here), [WHOLE, pl.BlockSpec(memory_space=pl.ANY)], name="split"
-    )
-    parts = [shifted(part, "pp", 1) for part in parts]
+    q = shifted(queries, "pp", 1)
     pairs = [pair] + [shifted(pair, "cp", d) for d in range(1, sources)]
-    bias = call(
+    features = call(
         prepare,
-        shape((sources * rows, rows), F32),
+        shape((2, sources * rows, LANES), BF16),
         (block_order, pair),
         [SCALARS, pl.BlockSpec(memory_space=pl.ANY)],
         name="prepare",
         micros=4,
     )
-    scaled, before = [], ()
-    for c in range(CHUNKS):
-        first = c * part_width // DH
-        part, *before = call(
-            functools.partial(attend, first, heads, sources),
-            (
-                shape((rows, part_width), BF16),
-                shape((8, rows), F32),
-                shape((1, first + part_width // DH), F32),
-            ),
-            (parts[c], norm_gain, bias, *pairs, *before),
-            scratch=[pltpu.VMEM((sources * rows, kv_width), BF16), pltpu.VMEM((kv_width, sources * rows), BF16)],
-            name="attend",
-            micros=1.5,
-        )
-        scaled.append(part)
-    squares, peak = before
+    scaled, squares, peak = call(
+        functools.partial(attend, sources),
+        (shape((rows, width), BF16), shape((8, rows), F32), shape((1, heads), F32)),
+        (q, norm_gain, features, *pairs),
+        scratch=[pltpu.VMEM((2, sources * rows, DH + LANES), BF16), pltpu.VMEM((DH + 16, sources * rows), BF16)],
+        limit=28,
+        name="attend",
+        micros=3,
+    )
     slab = shape((peers // 2, rows + SQUARE_ROWS, out_cols), BF16)
-    give, keep = call(project, (slab, slab), (kv_weight[0], squares, *scaled), name="project", micros=1)
+    give, keep = call(project, (slab, slab), (kv_weight[0], squares, scaled), name="project", micros=1)
     peak = bind(peak, give)
     got = lax.ppermute(give, "tp", [(i, i ^ 1) for i in range(peers)])
     slab = (rows + SQUARE_ROWS, out_cols)

time: 37.1 us -> 43.3 us (1.17)
  waiting for transfers between devices: 9.8 us -> 21.6 us
  starting transfers between devices: 17 us -> 13.4 us
  local copies, waits for them, and re-layouts: 3.24 us -> 0.66 us
  other arithmetic: 0 us -> 0.78 us
    ppermute x7 -> x6, waiting for transfers between devices: 6.55 us -> 16.4 us  [shifted(): lax.ppermute(block, axis, [((i - distance) % size, i) for i in range(size)])]
    ppermute x7 -> x6, starting transfers between devices: 10.7 us -> 8.84 us  [shifted(): lax.ppermute(block, axis, [((i - distance) % size, i) for i in range(size)])]
    unnamed x9 -> x6, local copies, waits for them, and re-layouts: 2.47 us -> 0.66 us
    ppermute x1, waiting for transfers between devices: 1.4 us -> 2.87 us  [returned(): return lax.ppermute(block, ('pp', 'cp'), route)]
    ppermute x1, starting transfers between devices: 2.05 us -> 0.74 us  [returned(): return lax.ppermute(block, ('pp', 'cp'), route)]
    another operation x0 -> x1, other arithmetic: none -> 0.78 us  [on_device(): pair_here = jnp.stack([key_vectors[0], value_vectors[0]])]
    concatenate x1 -> x0, local copies, waits for them, and re-layouts: 0.77 us -> none  [on_device(): pair_here = jnp.concatenate([key_vectors, value_vectors])]
    ppermute x1, waiting for transfers between devices: 1.85 us -> 2.29 us  [swapped(): lax.ppermute(block, axis, [(i, partner(i, step, size)) for i in range(siz...]
  transfers between devices with their start and end apart: 11 -> 10, of which waited for: 6 -> 5; matrix products, arithmetic and copies ran while one was open for 0% -> 2% of each run, Pallas kernels for 7% -> 1%
where the time goes in v1:
time: 43.3 us; the launch traced here: 43.1 us
  waiting for transfers between devices  21.6 us (50%)
  starting transfers between devices  13.4 us (31%)
  Pallas kernels  5.99 us (14%)
  other arithmetic  0.78 us (2%)
  between operations  0.71 us (2%)
  local copies, waits for them, and re-layouts  0.66 us (2%)
    ppermute x6, waiting for transfers between devices, shifted(): lax.ppermute(block, axis, [((i - distance) % size, i) for i in range(size)])  16.4 us
    ppermute x6, starting transfers between devices, shifted(): lax.ppermute(block, axis, [((i - distance) % size, i) for i in range(size)])  8.84 us
    pallas_call x6, Pallas kernels, call(): pl.pallas_call(kernel, out_shape=outs, in_specs=specs or [WHOLE] * len(ar...  5.99 us
    ppermute x1, waiting for transfers between devices, returned(): return lax.ppermute(block, ('pp', 'cp'), route)  2.87 us
    ppermute x1, waiting for transfers between devices, swapped(): lax.ppermute(block, axis, [(i, partner(i, step, size)) for i in range(siz...  2.29 us
    ppermute x1, starting transfers between devices, swapped(): lax.ppermute(block, axis, [(i, partner(i, step, size)) for i in range(siz...  2.15 us
    ppermute x1, starting transfers between devices, on_device(): lax.ppermute(block, 'tp', [(i, (i + 2 * (step + 1)) % peers) for i in ran...  1.58 us
  transfers between devices with their start and end apart: 10, of which 5 were waited for; matrix products, arithmetic and copies ran while one was open for 2% of the time, Pallas kernels for 1%

profile of v1, /device:TPU:0, one launch (start us, length us, event | category | flops | bytes accessed | tf_op | source)
XLA Modules:
  0.0 43.1 jit_solution(11738384487709923960)
XLA Ops:
  0.6 3.0 %collective-permute-start = (bf16[1,128,2048]{2,1,0:T(8,128)(2,1)}, bf16[1,128,2048]{2,1,0:T(8,128)(2,1)S(1)}, u32[]{:S(2)}, u32[]{:S(2)}) collective-permute-start(bf16[1,128,2048]{2,1,0:T(8,128)(2,1)} %param.6), channel_id=1, source_target_pairs={{16,0},{0,16},{17,1},{1,17},{18,2},{2,18},{19,3},{3,19},{20,4},{4,... | collective-permute-start | bytes 1572872 | tf_op jit(solution)/shard_map/ppermute | solution.py:163
  3.6 0.8 %pad_maximum_fusion = bf16[2,128,128]{2,1,0:T(8,128)(2,1)S(1)} fusion(bf16[1,128,128]{2,1,0:T(8,128)(2,1)} %param.8, bf16[1,128,128]{2,1,0:T(8,128)(2,1)} %param.7), kind=kLoop, calls=%fused_computation | loop fusion | flops 32768 | bytes 131072 | tf_op jit(solution)/shard_map/stack | solution.py:196
  4.4 0.1 collective-permute-start.1
  4.5 12.7 %collective-permute-done.1.after.refs_0_ = bf16[2,128,128]{2,1,0:T(8,128)(2,1)S(1)} collective-permute-done((bf16[2,128,128]{2,1,0:T(8,128)(2,1)S(1)}, bf16[2,128,128]{2,1,0:T(8,128)(2,1)S(1)}, u32[]{:S(2)}, u32[]{:S(2)}) %collective-permute-start.1) | collective-permute-done | bytes 65568 | tf_op jit(solution)/shard_map/ppermute | solution.py:163
  17.2 3.9 %collective-permute-start.4 = (bf16[2,128,128]{2,1,0:T(8,128)(2,1)S(1)}, bf16[2,128,128]{2,1,0:T(8,128)(2,1)S(1)}, u32[]{:S(2)}, u32[]{:S(2)}) collective-permute-start(bf16[2,128,128]{2,1,0:T(8,128)(2,1)S(1)} %collective-permute-done.1.after.refs_0_), channel_id=1, source_target_pairs={{4,0},{8,4},{12,8},{0,12},{5,1},{9,5},{13,9},{1,13},{6,2},{10,6},{... | collective-permute-start | bytes 196616 | tf_op jit(solution)/shard_map/ppermute | solution.py:163
  21.0 0.0 collective-permute-start.3
  21.0 1.0 %collective-permute-start.2 = (bf16[2,128,128]{2,1,0:T(8,128)(2,1)S(1)}, bf16[2,128,128]{2,1,0:T(8,128)(2,1)S(1)}, u32[]{:S(2)}, u32[]{:S(2)}) collective-permute-start(bf16[2,128,128]{2,1,0:T(8,128)(2,1)S(1)} %collective-permute-done.1.after.refs_0_), channel_id=1, source_target_pairs={{12,0},{0,4},{4,8},{8,12},{13,1},{1,5},{5,9},{9,13},{14,2},{2,6},{... | collective-permute-start | bytes 196616 | tf_op jit(solution)/shard_map/ppermute | solution.py:163
  22.0 0.7 %copy-done.2 = s32[8]{0:T(128)S(1)} copy-done((s32[8]{0:T(128)S(1)}, s32[8]{0:T(128)}, u32[]{:S(2)}) %copy-start.2) | copy-done | bytes 56
  22.7 0.6 %prepare.1.feature_ref = bf16[2,512,128]{2,1,0:T(8,128)(2,1)S(1)} custom-call(s32[8]{0:T(128)S(1)} %copy-done.2, bf16[2,128,128]{2,1,0:T(8,128)(2,1)S(1)} %collective-permute-done.1.after.refs_0_), custom_call_target="tpu_custom_call" | custom-call | flops 4000000000 | tf_op jit(solution)/shard_map/prepare/pallas_call | solution.py:23
  23.3 0.0 copy-start
  23.3 0.0 collective-permute-done.4.refs_3_
  23.3 2.8 %collective-permute-done.3.refs_2_ = bf16[2,128,128]{2,1,0:T(8,128)(2,1)S(1)} collective-permute-done((bf16[2,128,128]{2,1,0:T(8,128)(2,1)S(1)}, bf16[2,128,128]{2,1,0:T(8,128)(2,1)S(1)}, u32[]{:S(2)}, u32[]{:S(2)}) %collective-permute-start.3) | collective-permute-done | bytes 65568 | tf_op jit(solution)/shard_map/ppermute | solution.py:163
  26.2 0.9 %collective-permute-done.2.refs_1_ = bf16[2,128,128]{2,1,0:T(8,128)(2,1)S(1)} collective-permute-done((bf16[2,128,128]{2,1,0:T(8,128)(2,1)S(1)}, bf16[2,128,128]{2,1,0:T(8,128)(2,1)S(1)}, u32[]{:S(2)}, u32[]{:S(2)}) %collective-permute-start.2) | collective-permute-done | bytes 65568 | tf_op jit(solution)/shard_map/ppermute | solution.py:163
  27.1 0.0 collective-permute-done.q_ref
  27.1 3.7 %attend.1 = (bf16[128,2048]{1,0:T(8,128)(2,1)S(1)}, f32[8,128]{1,0:T(8,128)S(1)}, f32[1,16]{1,0:T(1,128)S(1)}) custom-call(bf16[1,128,2048]{2,1,0:T(8,128)(2,1)S(1)} %collective-permute-done.q_ref, bf16[1,2048]{1,0:T(2,128)(2,1)S(1)} %copy-done.1, bf16[2,512,128]{2,1,0:T(8,128)(2,1)S(1)} %prepare.1.feature_ref, ...), custom_call_target="tpu_custom_call" | custom-call | flops 3000000000 | tf_op jit(solution)/shard_map/attend/pallas_call | solution.py:23
  30.8 0.8 %project.1 = (bf16[2,144,256]{2,1,0:T(8,128)(2,1)S(1)}, bf16[2,144,256]{2,1,0:T(8,128)(2,1)S(1)}) custom-call(bf16[2048,1024]{1,0:T(8,128)(2,1)S(1)} %bitcast.2, f32[8,128]{1,0:T(8,128)S(1)} %get-tuple-element.12.square_ref, bf16[128,2048]{1,0:T(8,128)(2,1)S(1)} %get-tuple-element.13.scaled_ref), custom_call_target="tpu_custom_call" | custom-call | flops 1000000000 | tf_op jit(solution)/shard_map/project/pallas_call | solution.py:23
  31.6 0.1 collective-permute-start.5
  31.7 0.7 %collective-permute-start.7 = (f32[1,16]{1,0:T(1,128)S(1)}, f32[1,16]{1,0:T(1,128)S(1)}, u32[]{:S(2)}, u32[]{:S(2)}) collective-permute-start(f32[1,16]{1,0:T(1,128)S(1)} %bind.1), channel_id=1, source_target_pairs={{0,20},{4,16},{8,28},{12,24},{16,4},{20,0},{24,12},{28,8},{1,21},{... | collective-permute-start | bytes 200 | tf_op jit(solution)/shard_map/ppermute | solution.py:182
  32.4 0.9 %collective-permute-start.6 = (f32[1,16]{1,0:T(1,128)S(1)}, f32[1,16]{1,0:T(1,128)S(1)}, u32[]{:S(2)}, u32[]{:S(2)}) collective-permute-start(f32[1,16]{1,0:T(1,128)S(1)} %bind.1), channel_id=1, source_target_pairs={{16,0},{0,16},{17,1},{1,17},{18,2},{2,18},{19,3},{3,19},{20,4},{4,... | collective-permute-start | bytes 200 | tf_op jit(solution)/shard_map/ppermute | solution.py:163
  33.3 2.9 %collective-permute-done.7.peak_got = f32[1,16]{1,0:T(1,128)S(1)} collective-permute-done((f32[1,16]{1,0:T(1,128)S(1)}, f32[1,16]{1,0:T(1,128)S(1)}, u32[]{:S(2)}, u32[]{:S(2)}) %collective-permute-start.7) | collective-permute-done | bytes 96 | tf_op jit(solution)/shard_map/ppermute | solution.py:182
  36.3 1.6 %collective-permute-start.9 = (bf16[144,256]{1,0:T(8,128)(2,1)S(1)}, bf16[144,256]{1,0:T(8,128)(2,1)S(1)}, u32[]{:S(2)}, u32[]{:S(2)}) collective-permute-start(bf16[144,256]{1,0:T(8,128)(2,1)S(1)} %get-tuple-element.19), channel_id=1, source_target_pairs={{0,2},{1,3},{2,0},{3,1},{4,6},{5,7},{6,4},{7,5},{8,10},{9,11},{10,... | collective-permute-start | bytes 221192 | tf_op jit(solution)/shard_map/ppermute | solution.py:231
  37.9 2.1 %collective-permute-start.8 = (f32[1,16]{1,0:T(1,128)S(1)}, f32[1,16]{1,0:T(1,128)S(1)}, u32[]{:S(2)}, u32[]{:S(2)}) collective-permute-start(f32[1,16]{1,0:T(1,128)S(1)} %get-tuple-element.17.peak_ref), channel_id=1, source_target_pairs={{0,8},{4,12},{8,0},{12,4},{1,9},{5,13},{9,1},{13,5},{2,10},{6,14},... | collective-permute-start | bytes 200 | tf_op jit(solution)/shard_map/ppermute | solution.py:172
  40.0 2.3 %collective-permute-done.8.peak_got = f32[1,16]{1,0:T(1,128)S(1)} collective-permute-done((f32[1,16]{1,0:T(1,128)S(1)}, f32[1,16]{1,0:T(1,128)S(1)}, u32[]{:S(2)}, u32[]{:S(2)}) %collective-permute-start.8) | collective-permute-done | bytes 96 | tf_op jit(solution)/shard_map/ppermute | solution.py:172
  42.3 0.8 %finish.1 = (f32[1,16]{1,0:T(1,128)}, bf16[128,256]{1,0:T(8,128)(2,1)}) custom-call(f32[1,16]{1,0:T(1,128)S(1)} %get-tuple-element.17.peak_ref, f32[1,16]{1,0:T(1,128)S(1)} %collective-permute-done.8.peak_got, f32[144,256]{1,0:T(8,128)S(1)} %get-tuple-element.18.keep_ref, bf16[144,256]{1,0:T(8,128)(2,1)S(1)} %collective-permute-done.9.refs_0_), custom_call_target="tpu_custom_call" | custom-call | tf_op jit(solution)/shard_map/finish/pallas_call | solution.py:23
  (9 shorter events, 0.1 us)
Async XLA Ops:
  0.6 26.5 %collective-permute-start = (bf16[1,128,2048]{2,1,0:T(8,128)(2,1)}, bf16[1,128,2048]{2,1,0:T(8,128)(2,1)S(1)}, u32[]{:S(2)}, u32[]{:S(2)}) collective-permute-start(bf16[1,128,2048]{2,1,0:T(8,128)(2,1)} %param.6), channel_id=1, source_target_pairs={{16,0},{0,16},{17,1},{1,17},{18,2},{2,18},{19,3},{3,19},{20,4},{4,... | collective-permute-start | bytes 1572872 | tf_op jit(solution)/shard_map/ppermute | solution.py:163
  4.4 22.7 %copy-start.1 = (bf16[1,2048]{1,0:T(2,128)(2,1)S(1)}, bf16[1,2048]{1,0:T(2,128)(2,1)}, u32[]{:S(2)}) copy-start(bf16[1,2048]{1,0:T(2,128)(2,1)} %gain_ref.1) | copy-start | bytes 12292
  4.4 12.8 %collective-permute-start.1 = (bf16[2,128,128]{2,1,0:T(8,128)(2,1)S(1)}, bf16[2,128,128]{2,1,0:T(8,128)(2,1)S(1)}, u32[]{:S(2)}, u32[]{:S(2)}) collective-permute-start(bf16[2,128,128]{2,1,0:T(8,128)(2,1)S(1)} %pad_maximum_fusion), channel_id=1, source_target_pairs={{16,0},{0,16},{17,1},{1,17},{18,2},{2,18},{19,3},{3,19},{20,4},{4,... | collective-permute-start | bytes 196616 | tf_op jit(solution)/shard_map/ppermute | solution.py:163
  17.2 6.2 %collective-permute-start.4 = (bf16[2,128,128]{2,1,0:T(8,128)(2,1)S(1)}, bf16[2,128,128]{2,1,0:T(8,128)(2,1)S(1)}, u32[]{:S(2)}, u32[]{:S(2)}) collective-permute-start(bf16[2,128,128]{2,1,0:T(8,128)(2,1)S(1)} %collective-permute-done.1.after.refs_0_), channel_id=1, source_target_pairs={{4,0},{8,4},{12,8},{0,12},{5,1},{9,5},{13,9},{1,13},{6,2},{10,6},{... | collective-permute-start | bytes 196616 | tf_op jit(solution)/shard_map/ppermute | solution.py:163
  21.0 5.2 %collective-permute-start.3 = (bf16[2,128,128]{2,1,0:T(8,128)(2,1)S(1)}, bf16[2,128,128]{2,1,0:T(8,128)(2,1)S(1)}, u32[]{:S(2)}, u32[]{:S(2)}) collective-permute-start(bf16[2,128,128]{2,1,0:T(8,128)(2,1)S(1)} %collective-permute-done.1.after.refs_0_), channel_id=1, source_target_pairs={{8,0},{12,4},{0,8},{4,12},{9,1},{13,5},{1,9},{5,13},{10,2},{14,6},... | collective-permute-start | bytes 196616 | tf_op jit(solution)/shard_map/ppermute | solution.py:163
  21.0 6.1 %collective-permute-start.2 = (bf16[2,128,128]{2,1,0:T(8,128)(2,1)S(1)}, bf16[2,128,128]{2,1,0:T(8,128)(2,1)S(1)}, u32[]{:S(2)}, u32[]{:S(2)}) collective-permute-start(bf16[2,128,128]{2,1,0:T(8,128)(2,1)S(1)} %collective-permute-done.1.after.refs_0_), channel_id=1, source_target_pairs={{12,0},{0,4},{4,8},{8,12},{13,1},{1,5},{5,9},{9,13},{14,2},{2,6},{... | collective-permute-start | bytes 196616 | tf_op jit(solution)/shard_map/ppermute | solution.py:163
  22.0 0.7 %copy-start.2 = (s32[8]{0:T(128)S(1)}, s32[8]{0:T(128)}, u32[]{:S(2)}) copy-start(s32[8]{0:T(128)} %order_ref.1) | copy-start | bytes 100
  23.3 7.5 %copy-start = (bf16[1,2048,1024]{2,1,0:T(8,128)(2,1)S(1)}, bf16[1,2048,1024]{2,1,0:T(8,128)(2,1)}, u32[]{:S(2)}) copy-start(bf16[1,2048,1024]{2,1,0:T(8,128)(2,1)} %param.11) | copy-start | bytes 12582916
  31.6 4.6 %collective-permute-start.5 = (bf16[2,144,256]{2,1,0:T(8,128)(2,1)S(1)}, bf16[2,144,256]{2,1,0:T(8,128)(2,1)S(1)}, u32[]{:S(2)}, u32[]{:S(2)}) collective-permute-start(bf16[2,144,256]{2,1,0:T(8,128)(2,1)S(1)} %get-tuple-element.15.refs_0_), channel_id=1, source_target_pairs={{0,1},{1,0},{2,3},{3,2},{4,5},{5,4},{6,7},{7,6},{8,9},{9,8},{10,11... | collective-permute-start | bytes 442376 | tf_op jit(solution)/shard_map/ppermute | solution.py:220
  31.7 4.5 %collective-permute-start.7 = (f32[1,16]{1,0:T(1,128)S(1)}, f32[1,16]{1,0:T(1,128)S(1)}, u32[]{:S(2)}, u32[]{:S(2)}) collective-permute-start(f32[1,16]{1,0:T(1,128)S(1)} %bind.1), channel_id=1, source_target_pairs={{0,20},{4,16},{8,28},{12,24},{16,4},{20,0},{24,12},{28,8},{1,21},{... | collective-permute-start | bytes 200 | tf_op jit(solution)/shard_map/ppermute | solution.py:182
  32.4 3.8 %collective-permute-start.6 = (f32[1,16]{1,0:T(1,128)S(1)}, f32[1,16]{1,0:T(1,128)S(1)}, u32[]{:S(2)}, u32[]{:S(2)}) collective-permute-start(f32[1,16]{1,0:T(1,128)S(1)} %bind.1), channel_id=1, source_target_pairs={{16,0},{0,16},{17,1},{1,17},{18,2},{2,18},{19,3},{3,19},{20,4},{4,... | collective-permute-start | bytes 200 | tf_op jit(solution)/shard_map/ppermute | solution.py:163
  36.3 6.0 %collective-permute-start.9 = (bf16[144,256]{1,0:T(8,128)(2,1)S(1)}, bf16[144,256]{1,0:T(8,128)(2,1)S(1)}, u32[]{:S(2)}, u32[]{:S(2)}) collective-permute-start(bf16[144,256]{1,0:T(8,128)(2,1)S(1)} %get-tuple-element.19), channel_id=1, source_target_pairs={{0,2},{1,3},{2,0},{3,1},{4,6},{5,7},{6,4},{7,5},{8,10},{9,11},{10,... | collective-permute-start | bytes 221192 | tf_op jit(solution)/shard_map/ppermute | solution.py:231
  37.9 4.4 %collective-permute-start.8 = (f32[1,16]{1,0:T(1,128)S(1)}, f32[1,16]{1,0:T(1,128)S(1)}, u32[]{:S(2)}, u32[]{:S(2)}) collective-permute-start(f32[1,16]{1,0:T(1,128)S(1)} %get-tuple-element.17.peak_ref), channel_id=1, source_target_pairs={{0,8},{4,12},{8,0},{12,4},{1,9},{5,13},{9,1},{13,5},{2,10},{6,14},... | collective-permute-start | bytes 200 | tf_op jit(solution)/shard_map/ppermute | solution.py:172
